TPU v7x, 32 devices: a whole 2x2x4 slice. The times are simulated.
32 devices in a mesh: rep: 16 (over z, x, core), shard: 2 (over y).
Axes of the slice: x: 2, y: 2, z: 4, core: 2. Of those that a mesh axis runs over, the one named last changes fastest.
Arguments:
- tokens: bfloat16 [32768, 768], P(('rep', 'shard')), may hold values from -6 to 6
- cotangent: bfloat16 [32768, 768], P(('rep', 'shard')), may hold values from -6 to 6
- lengths: int32 [32], P(('rep', 'shard')), may hold values from 128 to 1024, as said below
- w_qkv: bfloat16 [768, 2304], P('shard'), may hold values from -0.21875 to 0.21875
- w_out: bfloat16 [768, 768], P('shard'), may hold values from -3.5 to 3.5
- w_up: bfloat16 [768, 3072], P('shard'), may hold values from -0.21875 to 0.21875
- w_down: bfloat16 [3072, 768], P('shard'), may hold values from -0.109375 to 0.109375
- norm_gains: bfloat16 [2, 768], P(None, 'shard'), may hold values from 0.5 to 1.5
- biases: bfloat16 [6, 768], P(None, 'shard'), may hold values from -3 to 3
- up_bias: bfloat16 [3072], P('shard'), may hold values from -3 to 3
Outputs:
- encoded: bfloat16 [32768, 768], P(('rep', 'shard'))
- grad_tokens: bfloat16 [32768, 768], P(('rep', 'shard'))
- grad_qkv: float32 [768, 2304], P('shard')
- grad_out: float32 [768, 768], P('shard')
- grad_up: float32 [768, 3072], P('shard')
- grad_down: float32 [3072, 768], P('shard')
- grad_gains: float32 [2, 768], P(None, 'shard')
- grad_biases: float32 [6, 768], P(None, 'shard')
- grad_up_bias: float32 [3072], P('shard')
Inputs may be any that keep to these rules, and one draw needn't show every extreme that they name: Each sequence has lengths live tokens at the start of its 1024 slots; some sequence has exactly 1024.
All inputs are finite; a program needn't handle non-finite values.
Results may differ from a plain program's by a relative error of at most 0.02.
Values may be sent and summed in bfloat16 or wider, within the bound.
A program may use at most 192 MiB of HBM per device.

v0:
```python
import jax
import jax.numpy as jnp
from jax import lax
from jax.sharding import PartitionSpec as P

HEADS = 12
HEAD_DIM = 64


epsilon = 1e-12
masked_score = -1000000000.0


def norm_forward(resid, gain_row, shift_row):
    center = resid - jnp.mean(resid, -1, keepdims=True)
    rstd_rows = lax.rsqrt(jnp.mean(center * center, -1, keepdims=True) + epsilon)
    normed = center * rstd_rows
    return (normed * gain_row + shift_row, normed, rstd_rows)


def norm_backward(grad_in, normed, rstd_rows, gain_row):
    scaled = grad_in * gain_row
    inner_term = (
        scaled
        - jnp.mean(scaled, -1, keepdims=True)
        - normed * jnp.mean(scaled * normed, -1, keepdims=True)
    )
    return (rstd_rows * inner_term, jnp.sum(grad_in * normed, 0), jnp.sum(grad_in, 0))


def gelu_exact(values):
    return jax.nn.gelu(values, approximate=False)


def block_scores(query_block, keys_seq, key_live, score_scale):
    scores = (
        jnp.einsum("qhd,khd->hqk", query_block, keys_seq, preferred_element_type=jnp.float32)
        * score_scale
    )
    return jnp.where(key_live[None, None, :], scores, masked_score)


def slot_forward(queries, keys_seq, values_seq, key_live):
    seq_len = queries.shape[0]
    block_rows = min(512, seq_len)
    score_scale = queries.shape[-1] ** (-0.5)
    grouped = queries.reshape(seq_len // block_rows, block_rows, queries.shape[1], queries.shape[2])

    def one_block(query_block):
        scores = block_scores(query_block, keys_seq, key_live, score_scale)
        row_top = jnp.max(scores, -1, keepdims=True)
        exponent = jnp.exp(scores - row_top)
        row_total = jnp.sum(exponent, -1, keepdims=True)
        probs_low = (exponent / row_total).astype(jnp.bfloat16)
        mixed_out = jnp.einsum(
            "hqk,khd->qhd", probs_low, values_seq, preferred_element_type=jnp.float32
        )
        return (mixed_out, (row_top + jnp.log(row_total))[..., 0])

    mixed_out, log_total = lax.map(one_block, grouped)
    return (mixed_out.reshape(seq_len, -1), log_total)


def slot_backward(queries, keys_seq, values_seq, key_live, log_total, grad_mixed):
    seq_len = queries.shape[0]
    block_rows = min(512, seq_len)
    block_count = seq_len // block_rows
    score_scale = queries.shape[-1] ** (-0.5)
    query_blocks = queries.reshape(block_count, block_rows, queries.shape[1], queries.shape[2])
    grad_blocks = grad_mixed.reshape(block_count, block_rows, queries.shape[1], queries.shape[2])

    def one_block(carried, block_item):
        grad_keys, grad_values = carried
        query_block, grad_block, total_block = block_item
        scores = block_scores(query_block, keys_seq, key_live, score_scale)
        probs = jnp.exp(scores - total_block[..., None])
        probs_low = probs.astype(jnp.bfloat16)
        grad_values = grad_values + jnp.einsum(
            "hqk,qhd->khd", probs_low, grad_block, preferred_element_type=jnp.float32
        )
        grad_probs = jnp.einsum(
            "qhd,khd->hqk", grad_block, values_seq, preferred_element_type=jnp.float32
        )
        row_inner = jnp.sum(probs * grad_probs, -1, keepdims=True)
        grad_scores = (probs * (grad_probs - row_inner)).astype(jnp.bfloat16)
        grad_query = (
            jnp.einsum("hqk,khd->qhd", grad_scores, keys_seq, preferred_element_type=jnp.float32)
            * score_scale
        )
        grad_keys = (
            grad_keys
            + jnp.einsum(
                "hqk,qhd->khd", grad_scores, query_block, preferred_element_type=jnp.float32
            )
            * score_scale
        )
        return ((grad_keys, grad_values), grad_query)

    empty_grad = jnp.zeros(keys_seq.shape, jnp.float32)
    (grad_keys, grad_values), grad_query = lax.scan(
        one_block, (empty_grad, empty_grad), (query_blocks, grad_blocks, log_total)
    )
    return (
        grad_query.reshape(seq_len, -1),
        grad_keys.reshape(seq_len, -1),
        grad_values.reshape(seq_len, -1),
    )


def per_device(tokens, cotangent, lengths, w_qkv, w_out, w_up, w_down, norm_gains, biases, up_bias):
    params_all = (w_qkv, w_out, w_up, w_down, norm_gains, biases, up_bias)
    gathered = (
        lax.all_gather(params_all[0], "shard", axis=0, tiled=True),
        lax.all_gather(params_all[1], "shard", axis=0, tiled=True),
        lax.all_gather(params_all[2], "shard", axis=0, tiled=True),
        lax.all_gather(params_all[3], "shard", axis=0, tiled=True),
        lax.all_gather(params_all[4], "shard", axis=1, tiled=True),
        lax.all_gather(params_all[5], "shard", axis=1, tiled=True),
        lax.all_gather(params_all[6], "shard", axis=0, tiled=True),
    )
    whole_qkv, whole_out, whole_up, whole_down, gain_all, bias_all, upb_all = gathered
    width = tokens.shape[1]
    slot_count = lengths.shape[0]
    seq_len = tokens.shape[0] // slot_count
    gain_f = gain_all.astype(jnp.float32)
    bias_f = bias_all.astype(jnp.float32)
    qkv_bias = jnp.concatenate([bias_f[0], jnp.zeros_like(bias_f[0]), bias_f[1]])
    qkv_low = (jnp.dot(tokens, whole_qkv, preferred_element_type=jnp.float32) + qkv_bias).astype(
        jnp.bfloat16
    )
    queries = qkv_low[:, :width].reshape(slot_count, seq_len, HEADS, HEAD_DIM)
    keys_all = qkv_low[:, width : 2 * width].reshape(slot_count, seq_len, HEADS, HEAD_DIM)
    values_all = qkv_low[:, 2 * width :].reshape(slot_count, seq_len, HEADS, HEAD_DIM)
    key_live = jnp.arange(seq_len, dtype=jnp.int32)[None, :] < lengths[:, None]
    attended, log_totals = lax.map(
        lambda slot_item: slot_forward(*slot_item), (queries, keys_all, values_all, key_live)
    )
    attended_low = attended.reshape(-1, width).astype(jnp.bfloat16)
    branch = jnp.dot(attended_low, whole_out, preferred_element_type=jnp.float32) + bias_f[2]
    normed_first, unit_first, rstd_first = norm_forward(
        tokens.astype(jnp.float32) + branch, gain_f[0], bias_f[4]
    )
    normed_low = normed_first.astype(jnp.bfloat16)
    hidden_pre = jnp.dot(normed_low, whole_up, preferred_element_type=jnp.float32) + upb_all.astype(
        jnp.float32
    )
    activated, gelu_pullback = jax.vjp(gelu_exact, hidden_pre)
    act_low = activated.astype(jnp.bfloat16)
    mlp_out = jnp.dot(act_low, whole_down, preferred_element_type=jnp.float32) + bias_f[3]
    result, unit_second, rstd_second = norm_forward(normed_first + mlp_out, gain_f[1], bias_f[5])
    encoded = result.astype(jnp.bfloat16)
    gathered = (
        lax.all_gather(params_all[0], "shard", axis=0, tiled=True),
        lax.all_gather(params_all[1], "shard", axis=0, tiled=True),
        lax.all_gather(params_all[2], "shard", axis=0, tiled=True),
        lax.all_gather(params_all[3], "shard", axis=0, tiled=True),
        lax.all_gather(params_all[4], "shard", axis=1, tiled=True),
        lax.all_gather(params_all[5], "shard", axis=1, tiled=True),
        lax.all_gather(params_all[6], "shard", axis=0, tiled=True),
    )
    whole_qkv, whole_out, whole_up, whole_down, gain_all, bias_all, upb_all = gathered
    gain_f = gain_all.astype(jnp.float32)
    d_second, d_gain_two, d_shift_two = norm_backward(
        cotangent.astype(jnp.float32), unit_second, rstd_second, gain_f[1]
    )
    d_mlp = d_second.astype(jnp.bfloat16)
    d_bias_down = jnp.sum(d_mlp.astype(jnp.float32), 0)
    grad_down = jnp.einsum("tf,td->fd", act_low, d_mlp, preferred_element_type=jnp.float32)
    d_act = jnp.einsum("td,fd->tf", d_mlp, whole_down, preferred_element_type=jnp.float32)
    d_pre = gelu_pullback(d_act)[0].astype(jnp.bfloat16)
    grad_up_bias = jnp.sum(d_pre.astype(jnp.float32), 0)
    grad_up = jnp.einsum("td,tf->df", normed_low, d_pre, preferred_element_type=jnp.float32)
    d_normed = d_second + jnp.einsum(
        "tf,df->td", d_pre, whole_up, preferred_element_type=jnp.float32
    )
    d_first, d_gain_one, d_shift_one = norm_backward(d_normed, unit_first, rstd_first, gain_f[0])
    d_branch = d_first.astype(jnp.bfloat16)
    d_bias_out = jnp.sum(d_branch.astype(jnp.float32), 0)
    grad_out = jnp.einsum("ta,td->ad", attended_low, d_branch, preferred_element_type=jnp.float32)
    d_attended = jnp.einsum(
        "td,ad->ta", d_branch, whole_out, preferred_element_type=jnp.float32
    ).astype(jnp.bfloat16)
    d_attended = d_attended.reshape(slot_count, seq_len, HEADS, HEAD_DIM)
    grad_query, grad_keys, grad_values = lax.map(
        lambda slot_item: slot_backward(*slot_item),
        (queries, keys_all, values_all, key_live, log_totals, d_attended),
    )
    d_qkv = jnp.concatenate(
        [
            grad_query.reshape(-1, width),
            grad_keys.reshape(-1, width),
            grad_values.reshape(-1, width),
        ],
        axis=1,
    ).astype(jnp.bfloat16)
    d_qkv_sums = jnp.sum(d_qkv.astype(jnp.float32), 0)
    grad_qkv = jnp.einsum("td,te->de", tokens, d_qkv, preferred_element_type=jnp.float32)
    grad_tokens = (
        d_first + jnp.einsum("te,de->td", d_qkv, whole_qkv, preferred_element_type=jnp.float32)
    ).astype(jnp.bfloat16)
    grad_gains = jnp.stack([d_gain_one, d_gain_two])
    grad_biases = jnp.stack(
        [
            d_qkv_sums[:width],
            d_qkv_sums[2 * width :],
            d_bias_out,
            d_bias_down,
            d_shift_one,
            d_shift_two,
        ]
    )
    local_grads = (grad_qkv, grad_out, grad_up, grad_down, grad_gains, grad_biases, grad_up_bias)
    owned = (
        lax.psum_scatter(
            local_grads[0].astype(jnp.bfloat16), "shard", scatter_dimension=0, tiled=True
        ).astype(jnp.float32),
        lax.psum_scatter(
            local_grads[1].astype(jnp.bfloat16), "shard", scatter_dimension=0, tiled=True
        ).astype(jnp.float32),
        lax.psum_scatter(
            local_grads[2].astype(jnp.bfloat16), "shard", scatter_dimension=0, tiled=True
        ).astype(jnp.float32),
        lax.psum_scatter(
            local_grads[3].astype(jnp.bfloat16), "shard", scatter_dimension=0, tiled=True
        ).astype(jnp.float32),
        lax.psum_scatter(
            local_grads[4].astype(jnp.bfloat16), "shard", scatter_dimension=1, tiled=True
        ).astype(jnp.float32),
        lax.psum_scatter(
            local_grads[5].astype(jnp.bfloat16), "shard", scatter_dimension=1, tiled=True
        ).astype(jnp.float32),
        lax.psum_scatter(
            local_grads[6].astype(jnp.bfloat16), "shard", scatter_dimension=0, tiled=True
        ).astype(jnp.float32),
    )
    summed = (
        lax.psum(owned[0].astype(jnp.bfloat16), "rep").astype(jnp.float32),
        lax.psum(owned[1].astype(jnp.bfloat16), "rep").astype(jnp.float32),
        lax.psum(owned[2].astype(jnp.bfloat16), "rep").astype(jnp.float32),
        lax.psum(owned[3].astype(jnp.bfloat16), "rep").astype(jnp.float32),
        lax.psum(owned[4].astype(jnp.bfloat16), "rep").astype(jnp.float32),
        lax.psum(owned[5].astype(jnp.bfloat16), "rep").astype(jnp.float32),
        lax.psum(owned[6].astype(jnp.bfloat16), "rep").astype(jnp.float32),
    )
    return (
        encoded,
        grad_tokens,
        summed[0],
        summed[1],
        summed[2],
        summed[3],
        summed[4],
        summed[5],
        summed[6],
    )


def solution(mesh):
    in_specs = (
        P(("rep", "shard"), None),
        P(("rep", "shard"), None),
        P(("rep", "shard")),
        P("shard", None),
        P("shard", None),
        P("shard", None),
        P("shard", None),
        P(None, "shard"),
        P(None, "shard"),
        P("shard"),
    )
    out_specs = (
        P(("rep", "shard"), None),
        P(("rep", "shard"), None),
        P("shard", None),
        P("shard", None),
        P("shard", None),
        P("shard", None),
        P(None, "shard"),
        P(None, "shard"),
        P("shard"),
    )
    return jax.shard_map(
        per_device, mesh=mesh, in_specs=in_specs, out_specs=out_specs, check_vma=False
    )
```

profile of v0, /device:TPU:0, one launch (start us, length us, event | category | flops | bytes accessed | tf_op | source)
XLA Modules:
  0.0 865.6 jit_solution(13616373402979181304)
XLA Ops:
  29.3 32.4 %all-gather.6.cloned.1.call-done = bf16[768,2304]{1,0:T(8,128)(2,1)} async-done(((bf16[384,2304]{1,0:T(8,128)(2,1)}), bf16[768,2304]{1,0:T(8,128)(2,1)}) %all-gather.6.cloned.1.call-update) | async-done | bytes 3538960 | tf_op jit(solution)/shard_map/all_gather | solution.py:113
  81.2 71.2 %while.48 = (s32[]{:T(128)}, bf16[2,512,12,64]{1,3,2,0:T(8,128)(2,1)}, f32[2,12,512]{2,1,0:T(8,128)S(1)}, bf16[2,512,12,64]{1,3,2,0:T(8,128)(2,1)S(1)}, bf16[102...) while((s32[]{:T(128)}, ...), condition=%wide.region_3.4_spmd.clone, body=%wide.region_0.3_spmd.clone.sunk | while | flops 1686105088 | bytes 100118728 | solution.py:60
  92.0 13.3 %fusion.107 = f32[12,512]{1,0:T(8,128)S(1)} fusion(f32[12,512,1024]{2,1,0:T(8,128)} %get-tuple-element.468, f32[12,512]{1,0:T(8,128)S(1)} %get-tuple-element.469, pred[1024]{0:T(1024)(128)(4,1)S(1)} %iota_compare_fusion.4), kind=kLoop, calls=%fused_computation.6.clone.1 | loop fusion | flops 25159680 | bytes 25216000 | tf_op jit(solution)/shard_map/while/body/eval_jaxpr/while/body/eval_jaxpr/reduce_sum | solution.py:53
  105.3 11.2 %bitcast_dynamic-update-slice_fusion.6 = bf16[2,512,12,64]{1,3,2,0:T(8,128)(2,1)S(1)} fusion(bf16[2,512,12,64]{1,3,2,0:T(8,128)(2,1)S(1)} %copy-done.18, s32[]{:T(128)S(6)} %copy.85, bf16[1024,12,64]{0,2,1:T(8,128)(2,1)S(1)} %copy-done.5, f32[12,512,1024]{2,1,0:T(8,128)} %get-tuple-element.468, f32[12,512]{1,0:T(8,128)S(1)} %fusion.107, ...), kind=kOutput, calls=%fused_computation.8.clone.1 | convolution fusion | flops 836763648 | bytes 28378116 | tf_op jit(solution)/shard_map/while/body/eval_jaxpr/while/body/eval_jaxpr/hqk,khd->qhd/dot_general | solution.py:55
  128.4 11.4 %fusion.107 = f32[12,512]{1,0:T(8,128)S(1)} fusion(f32[12,512,1024]{2,1,0:T(8,128)} %get-tuple-element.468, f32[12,512]{1,0:T(8,128)S(1)} %get-tuple-element.469, pred[1024]{0:T(1024)(128)(4,1)S(1)} %iota_compare_fusion.4), kind=kLoop, calls=%fused_computation.6.clone.1 | loop fusion | flops 25159680 | bytes 25216000 | tf_op jit(solution)/shard_map/while/body/eval_jaxpr/while/body/eval_jaxpr/reduce_sum | solution.py:53
  139.8 11.2 %bitcast_dynamic-update-slice_fusion.6 = bf16[2,512,12,64]{1,3,2,0:T(8,128)(2,1)S(1)} fusion(bf16[2,512,12,64]{1,3,2,0:T(8,128)(2,1)S(1)} %copy-done.18, s32[]{:T(128)S(6)} %copy.85, bf16[1024,12,64]{0,2,1:T(8,128)(2,1)S(1)} %copy-done.5, f32[12,512,1024]{2,1,0:T(8,128)} %get-tuple-element.468, f32[12,512]{1,0:T(8,128)S(1)} %fusion.107, ...), kind=kOutput, calls=%fused_computation.8.clone.1 | convolution fusion | flops 836763648 | bytes 28378116 | tf_op jit(solution)/shard_map/while/body/eval_jaxpr/while/body/eval_jaxpr/hqk,khd->qhd/dot_general | solution.py:55
  163.5 38.1 %multiply_convert_fusion.1 = (bf16[1024,3072]{1,0:T(8,128)(2,1)}, f32[1024,3072]{1,0:T(8,128)}, f32[1024,3072]{1,0:T(8,128)}) fusion(f32[3072]{0:T(1024)S(1)} %bitcast.141, bf16[768,3072]{1,0:T(8,128)(2,1)} %all-gather.10.cloned.1.call-done, f32[1024,768]{0,1:T(8,128)S(1)} %get-tuple-element.361, f32[768]{0:T(1024)S(1)} %copy-done.44, ...), kind=kOutput, calls=%fused_computation.47 | convolution fusion | flops 5043388416 | bytes 39348224 | tf_op jit(solution)/shard_map/dot_general | solution.py:144
  201.6 12.8 %all-gather.12.cloned.1.call-done = bf16[3072,768]{1,0:T(8,128)(2,1)} async-done(((bf16[1536,768]{1,0:T(8,128)(2,1)}), bf16[3072,768]{1,0:T(8,128)(2,1)}) %all-gather.12.cloned.1.call-update) | async-done | bytes 4718608 | tf_op jit(solution)/shard_map/all_gather | solution.py:116
  214.5 20.3 %fusion.63 = (f32[1024]{0:T(1024)S(1)}, f32[1024,768]{0,1:T(8,128)S(1)}) fusion(f32[768]{0:T(1024)S(1)} %copy-done.46, bf16[1024,3072]{1,0:T(8,128)(2,1)} %get-tuple-element.348, bf16[3072,768]{1,0:T(8,128)(2,1)} %all-gather.12.cloned.1.call-done, f32[768]{0:T(1024)S(1)} %copy-done.44, f32[768]{0:T(1024)S(1)} %copy-done.32, f32[1024]{0:T(1024)S(1)} %add_rsqrt_fusion.1, ...), kind=kOutput, calls=%fused_computation.121 | convolution fusion | flops 4837342208 | bytes 17323008 | tf_op jit(solution)/shard_map/dot_general | solution.py:149
  241.2 18.1 %fusion.64 = (bf16[3072]{0:T(1024)(128)(2,1)}, bf16[1024,3072]{1,0:T(8,128)(2,1)}) fusion(f32[1024,3072]{1,0:T(8,128)} %get-tuple-element.349, bf16[1024,768]{0,1:T(8,128)(2,1)S(1)} %get-tuple-element.345, bf16[3072,768]{1,0:T(8,128)(2,1)} %all-gather.12.cloned.1.call-done, f32[1024,3072]{1,0:T(8,128)} %get-tuple-element.362, f32[3072]{0:T(1024)S(1)} %bitcast.142), kind=kOutput, calls=%fused_computation.122 | convolution fusion | flops 4882166784 | bytes 37767168 | tf_op jit(solution)/shard_map/td,fd->tf/dot_general | solution.py:169
  259.3 11.5 %multiply_reduce_fusion.1 = (bf16[768]{0:T(1024)(128)(2,1)}, f32[1024]{0:T(1024)S(1)}, f32[1024]{0:T(1024)S(1)}, bf16[768]{0:T(1024)(128)(2,1)}, f32[1024,768]{0,1:T(8,128)S(1)}) fusion(f32[1024,768]{0,1:T(8,128)} %copy-done.8, f32[1024]{0:T(1024)S(1)} %add_rsqrt_fusion.1, f32[1024]{0:T(1024)S(1)} %broadcast_multiply_fusion.5, f32[768]{0:T(1024)S(1)} %copy-done.32, ...), kind=kOutput, calls=%fused_computation.76 | convolution fusion | flops 4845989888 | bytes 22062080 | tf_op jit(solution)/shard_map/tf,df->td/dot_general | solution.py:173
  283.3 163.3 %while.49 = (s32[]{:T(128)}, f32[1024,12,64]{0,2,1:T(8,128)}, f32[1024,12,64]{0,2,1:T(8,128)}, bf16[2,512,12,64]{1,3,2,0:T(8,128)(2,1)}, bf16[2,512,12,64]{1,3,2...) while((s32[]{:T(128)}, f32[1024,12,64]{0,2,1:T(8,128)}, ...), condition=%wide.region_14.15_spmd.clone, body=%wide.region_12.14_spmd.clone.sunk | while | flops 4125223936 | bytes 217239728 | solution.py:100
  294.5 12.9 %bitcast_add_fusion.5 = f32[1024,12,64]{0,2,1:T(8,128)} fusion(f32[1024,12,64]{0,2,1:T(8,128)} %get-tuple-element.520, f32[12,512,1024]{2,1,0:T(8,128)} %fusion.117, f32[12,512]{1,0:T(8,128)S(1)} %dynamic-slice_bitcast_fusion.2, pred[1024]{0:T(1024)(128)(4,1)S(1)} %iota_compare_fusion.5, pred[]{:T(512)S(6)} %compare.3, ...), kind=kOutput, calls=%fused_computation.23.clone.1 | convolution fusion | flops 832045056 | bytes 32277508 | tf_op jit(solution)/shard_map/while/body/eval_jaxpr/while/body/eval_jaxpr/hqk,qhd->khd/dot_general | solution.py:78
  307.4 17.4 %multiply_reduce_fusion.7 = (f32[12,512]{1,0:T(8,128)S(1)}, f32[12,512,1024]{2,1,0:T(8,128)}) fusion(f32[12,512,1024]{2,1,0:T(8,128)} %fusion.117, f32[12,512]{1,0:T(8,128)S(1)} %dynamic-slice_bitcast_fusion.2, pred[1024]{0:T(1024)(128)(4,1)S(1)} %iota_compare_fusion.5, bf16[1024,12,64]{0,2,1:T(8,128)(2,1)} %get-tuple-element.538, ...), kind=kOutput, calls=%fused_computation.18.clone.1 | convolution fusion | flops 836757504 | bytes 52741124 | tf_op jit(solution)/shard_map/while/body/eval_jaxpr/while/body/eval_jaxpr/qhd,khd->hqk/dot_general | solution.py:81
  324.8 21.5 %multiply_convert_fusion.3 = bf16[12,512,1024]{2,1,0:T(8,128)(2,1)} fusion(f32[12,512,1024]{2,1,0:T(8,128)} %get-tuple-element.480, f32[12,512,1024]{2,1,0:T(8,128)} %fusion.117, f32[12,512]{1,0:T(8,128)S(1)} %get-tuple-element.481, f32[12,512]{1,0:T(8,128)S(1)} %dynamic-slice_bitcast_fusion.2, pred[1024]{0:T(1024)(128)(4,1)S(1)} %iota_compare_fusion.5), kind=kLoop, calls=%fused_computation.17.clone.1 | loop fusion | flops 37748736 | bytes 62964736 | tf_op jit(solution)/shard_map/while/body/eval_jaxpr/while/body/eval_jaxpr/convert_element_type | solution.py:85
  375.0 13.8 %bitcast_add_fusion.5 = f32[1024,12,64]{0,2,1:T(8,128)} fusion(f32[1024,12,64]{0,2,1:T(8,128)} %get-tuple-element.520, f32[12,512,1024]{2,1,0:T(8,128)} %fusion.117, f32[12,512]{1,0:T(8,128)S(1)} %dynamic-slice_bitcast_fusion.2, pred[1024]{0:T(1024)(128)(4,1)S(1)} %iota_compare_fusion.5, pred[]{:T(512)S(6)} %compare.3, ...), kind=kOutput, calls=%fused_computation.23.clone.1 | convolution fusion | flops 832045056 | bytes 32277508 | tf_op jit(solution)/shard_map/while/body/eval_jaxpr/while/body/eval_jaxpr/hqk,qhd->khd/dot_general | solution.py:78
  388.8 17.4 %multiply_reduce_fusion.7 = (f32[12,512]{1,0:T(8,128)S(1)}, f32[12,512,1024]{2,1,0:T(8,128)}) fusion(f32[12,512,1024]{2,1,0:T(8,128)} %fusion.117, f32[12,512]{1,0:T(8,128)S(1)} %dynamic-slice_bitcast_fusion.2, pred[1024]{0:T(1024)(128)(4,1)S(1)} %iota_compare_fusion.5, bf16[1024,12,64]{0,2,1:T(8,128)(2,1)} %get-tuple-element.538, ...), kind=kOutput, calls=%fused_computation.18.clone.1 | convolution fusion | flops 836757504 | bytes 52741124 | tf_op jit(solution)/shard_map/while/body/eval_jaxpr/while/body/eval_jaxpr/qhd,khd->hqk/dot_general | solution.py:81
  406.2 21.5 %multiply_convert_fusion.3 = bf16[12,512,1024]{2,1,0:T(8,128)(2,1)} fusion(f32[12,512,1024]{2,1,0:T(8,128)} %get-tuple-element.480, f32[12,512,1024]{2,1,0:T(8,128)} %fusion.117, f32[12,512]{1,0:T(8,128)S(1)} %get-tuple-element.481, f32[12,512]{1,0:T(8,128)S(1)} %dynamic-slice_bitcast_fusion.2, pred[1024]{0:T(1024)(128)(4,1)S(1)} %iota_compare_fusion.5), kind=kLoop, calls=%fused_computation.17.clone.1 | loop fusion | flops 37748736 | bytes 62964736 | tf_op jit(solution)/shard_map/while/body/eval_jaxpr/while/body/eval_jaxpr/convert_element_type | solution.py:85
  499.7 14.0 %reduce-scatter.19.cloned.1.call-done = bf16[384,2304]{1,0:T(8,128)(2,1)} async-done(((bf16[768,2304]{1,0:T(8,128)(2,1)}), bf16[384,2304]{1,0:T(8,128)(2,1)}) %reduce-scatter.19.cloned.1.call-update) | async-done | bytes 1769488
  517.6 20.7 %reduce-scatter.13.cloned.1.call-done = bf16[384,768]{1,0:T(8,128)(2,1)} async-done(((bf16[768,768]{1,0:T(8,128)(2,1)}), bf16[384,768]{1,0:T(8,128)(2,1)}) %reduce-scatter.13.cloned.1.call-update) | async-done | bytes 589840 | tf_op jit(solution)/shard_map/reduce_scatter | solution.py:217
  538.3 62.9 %reduce-scatter.17.cloned.1.call-done = bf16[1536,768]{1,0:T(8,128)(2,1)} async-done(((bf16[3072,768]{1,0:T(8,128)(2,1)}), bf16[1536,768]{1,0:T(8,128)(2,1)}) %reduce-scatter.17.cloned.1.call-update) | async-done | bytes 2359312 | tf_op jit(solution)/shard_map/reduce_scatter | solution.py:223
  601.2 63.0 %reduce-scatter.15.cloned.1.call-done = bf16[384,3072]{1,0:T(8,128)(2,1)} async-done(((bf16[768,3072]{1,0:T(8,128)(2,1)}), bf16[384,3072]{1,0:T(8,128)(2,1)}) %reduce-scatter.15.cloned.1.call-update) | async-done | bytes 2359312 | tf_op jit(solution)/shard_map/reduce_scatter | solution.py:220
  691.5 64.1 %all-reduce.1 = (bf16[2,384]{1,0:T(2,128)(2,1)S(1)}, bf16[6,384]{1,0:T(8,128)(2,1)S(1)}, bf16[1536]{0:T(1024)(128)(2,1)S(1)}) all-reduce(bf16[2,384]{1,0:T(2,128)(2,1)S(1)} %copy.74, bf16[6,384]{1,0:T(8,128)(2,1)S(1)} %copy.76, bf16[1536]{0:T(1024)(128)(2,1)S(1)} %dynamic-slice.2), channel_id=1, replica_groups=mesh['rep'=16,'shard'=2] {'rep'}, use_global_device_ids=true, to_apply=%region_26.27 | all-reduce | flops 4608 | bytes 18432 | tf_op jit(solution)/shard_map/psum | solution.py:241
  757.3 89.9 %all-reduce.5.cloned.1.call-done = (bf16[384,2304]{0,1:T(8,128)(2,1)}, bf16[384,768]{1,0:T(8,128)(2,1)}, bf16[384,3072]{1,0:T(8,128)(2,1)}, bf16[1536,768]{1,0:T(8,128)(2,1)}) async-done(((bf16[384,2304]{0,1:T(8,128)(2,1)}, bf16[384,768]{1,0:T(8,128)(2,1)}, bf16[384,3072]{1,0:T(8,128)(2,1)}, bf16[1536,768]{1,0:T(8,128)(2,1)}), (bf16[384,2304]{0,1:T(8,128)(2,1)}, bf16[384,768]{1,0:T(8,128)(2,1)}, ...) | async-done | bytes 7077904 | tf_op jit(solution)/shard_map/psum | solution.py:237
  (240 shorter events, 249.9 us)
Async XLA Ops:
  7.2 13.8 %copy-start.42 = (bf16[6,384]{1,0:T(8,128)(2,1)S(1)}, bf16[6,384]{1,0:T(8,128)(2,1)}, u32[]{:S(2)}) copy-start(bf16[6,384]{1,0:T(8,128)(2,1)} %param.22) | copy-start | bytes 13828
  7.2 54.5 %all-gather.6.cloned.1.call-start = ((), (), s32[]{:S(2)}) async-start(), calls=%async_computation.6 | async-start | bytes 5308416 | tf_op jit(solution)/shard_map/all_gather | solution.py:113
  7.9 18.0 %copy-start.11 = (bf16[1024,768]{1,0:T(8,128)(2,1)S(1)}, bf16[1024,768]{1,0:T(8,128)(2,1)}, u32[]{:S(2)}) copy-start(bf16[1024,768]{1,0:T(8,128)(2,1)} %param.15) | copy-start | bytes 4718596
  8.0 150.3 %all-gather.8.cloned.1.call-start = ((), (), s32[]{:S(2)}) async-start(), calls=%async_computation.7 | async-start | bytes 1769472 | tf_op jit(solution)/shard_map/all_gather | solution.py:114
  8.7 154.5 %all-gather.10.cloned.1.call-start = ((), (), s32[]{:S(2)}) async-start(), calls=%async_computation.8 | async-start | bytes 7077888 | tf_op jit(solution)/shard_map/all_gather | solution.py:115
  9.4 18.1 %copy-start.24 = (bf16[1024,768]{1,0:T(8,128)(2,1)S(1)}, bf16[1024,768]{1,0:T(8,128)(2,1)}, u32[]{:S(2)}) copy-start(bf16[1024,768]{1,0:T(8,128)(2,1)} %param.14) | copy-start | bytes 4718596
  9.4 205.0 %all-gather.12.cloned.1.call-start = ((), (), s32[]{:S(2)}) async-start(), calls=%async_computation.9 | async-start | bytes 7077888 | tf_op jit(solution)/shard_map/all_gather | solution.py:116
  10.0 503.7 %reduce-scatter.19.cloned.1.call-start = ((), (), s32[]{:S(2)}) async-start(), calls=%async_computation.13 | async-start | bytes 5308416
  92.0 13.3 %copy-start.5 = (bf16[1024,12,64]{0,2,1:T(8,128)(2,1)S(1)}, bf16[1024,12,64]{0,2,1:T(8,128)(2,1)}, u32[]{:S(2)}) copy-start(bf16[1024,12,64]{0,2,1:T(8,128)(2,1)} %get-tuple-element.503) | copy-start | bytes 4718596 | tf_op jit(solution)/shard_map/while/body/eval_jaxpr/while
  92.0 13.3 %copy-start.18 = (bf16[2,512,12,64]{1,3,2,0:T(8,128)(2,1)S(1)}, bf16[2,512,12,64]{1,3,2,0:T(8,128)(2,1)}, u32[]{:S(2)}) copy-start(bf16[2,512,12,64]{1,3,2,0:T(8,128)(2,1)} %get-tuple-element.491) | copy-start | bytes 4718596 | tf_op jit(solution)/shard_map/while/body/eval_jaxpr/while
  128.4 11.4 %copy-start.5 = (bf16[1024,12,64]{0,2,1:T(8,128)(2,1)S(1)}, bf16[1024,12,64]{0,2,1:T(8,128)(2,1)}, u32[]{:S(2)}) copy-start(bf16[1024,12,64]{0,2,1:T(8,128)(2,1)} %get-tuple-element.503) | copy-start | bytes 4718596 | tf_op jit(solution)/shard_map/while/body/eval_jaxpr/while
  128.4 11.4 %copy-start.18 = (bf16[2,512,12,64]{1,3,2,0:T(8,128)(2,1)S(1)}, bf16[2,512,12,64]{1,3,2,0:T(8,128)(2,1)}, u32[]{:S(2)}) copy-start(bf16[2,512,12,64]{1,3,2,0:T(8,128)(2,1)} %get-tuple-element.491) | copy-start | bytes 4718596 | tf_op jit(solution)/shard_map/while/body/eval_jaxpr/while
  162.7 51.8 %copy-start.8 = (f32[1024,768]{0,1:T(8,128)}, f32[1024,768]{0,1:T(8,128)S(1)}, u32[]{:S(2)}) copy-start(f32[1024,768]{0,1:T(8,128)S(1)} %get-tuple-element.361) | copy-start | bytes 9437188
  162.8 108.0 %copy-start.29 = (f32[1024]{0:T(1024)}, f32[1024]{0:T(1024)S(1)}, u32[]{:S(2)}) copy-start(f32[1024]{0:T(1024)S(1)} %broadcast_multiply_fusion.5) | copy-start | bytes 12292
  163.2 107.6 %copy-start.34 = (f32[1024]{0:T(1024)}, f32[1024]{0:T(1024)S(1)}, u32[]{:S(2)}) copy-start(f32[1024]{0:T(1024)S(1)} %add_rsqrt_fusion.1) | copy-start | bytes 12292
  163.5 51.0 %copy-start.46 = (f32[768]{0:T(1024)S(1)}, f32[768]{0:T(1024)}, u32[]{:S(2)}) copy-start(f32[768]{0:T(1024)} %get-tuple-element.296) | copy-start | bytes 9220
  241.2 18.1 %copy-start.26 = (bf16[1024,768]{0,1:T(8,128)(2,1)}, bf16[1024,768]{0,1:T(8,128)(2,1)S(1)}, u32[]{:S(2)}) copy-start(bf16[1024,768]{0,1:T(8,128)(2,1)S(1)} %get-tuple-element.345) | copy-start | bytes 4718596
  259.3 11.5 %copy-start.9 = (f32[1024,768]{0,1:T(8,128)S(1)}, f32[1024,768]{0,1:T(8,128)}, u32[]{:S(2)}) copy-start(f32[1024,768]{0,1:T(8,128)} %copy-done.8) | copy-start | bytes 9437188
  465.9 72.4 %reduce-scatter.13.cloned.1.call-start = ((), (), s32[]{:S(2)}) async-start(), calls=%async_computation.10 | async-start | bytes 1769472 | tf_op jit(solution)/shard_map/reduce_scatter | solution.py:217
  471.7 129.5 %reduce-scatter.17.cloned.1.call-start = ((), (), s32[]{:S(2)}) async-start(), calls=%async_computation.12 | async-start | bytes 7077888 | tf_op jit(solution)/shard_map/reduce_scatter | solution.py:223
  481.7 182.6 %reduce-scatter.15.cloned.1.call-start = ((), (), s32[]{:S(2)}) async-start(), calls=%async_computation.11 | async-start | bytes 7077888 | tf_op jit(solution)/shard_map/reduce_scatter | solution.py:220
  493.7 191.1 %reduce-scatter.21.cloned.1.call-start = ((), (), s32[]{:S(2)}) async-start(), calls=%async_computation.14 | async-start | bytes 294912
  498.6 191.9 %reduce-scatter.23.cloned.1.call-start = ((), (), s32[]{:S(2)}) async-start(), calls=%async_computation.15 | async-start | bytes 294912
  499.7 347.6 %all-reduce.5.cloned.1.call-start = ((), (), s32[]{:S(2)}) async-start(), calls=%async_computation.16 | async-start | bytes 14155776 | tf_op jit(solution)/shard_map/psum | solution.py:237
  (44 other events, 148.2 us)
Sparse Core Ops, SparseCore 0:
  9.6 52.1 all-gather.5
  63.3 22.8 all-gather.7
  87.7 62.6 all-gather.9
  151.8 62.6 all-gather.11
  466.1 47.6 reduce-scatter.18
  516.5 21.7 reduce-scatter.12
  541.2 59.9 reduce-scatter.16
  604.2 60.0 reduce-scatter.14
  666.5 10.9 reduce-scatter.20
  679.5 10.9 reduce-scatter.22
  695.1 152.0 all-reduce.4
where the time goes:
time: 869 us; the launch traced here: 866 us
  waiting for transfers between devices  303 us (35%)
  matrix products  301 us (35%)
  other arithmetic  93.6 us (11%)
  blocking collectives  83 us (10%)
  local copies, waits for them, and re-layouts  68.3 us (8%)
  between operations  15.4 us (2%)
    psum x1, waiting for transfers between devices, per_device(): lax.psum(owned[0].astype(jnp.bfloat16), 'rep').astype(jnp.float32)  89.9 us
    psum x1, blocking collectives, per_device(): lax.psum(owned[4].astype(jnp.bfloat16), 'rep').astype(jnp.float32)  64.1 us
    reduce_scatter x1, waiting for transfers between devices, per_device(): lax.psum_scatter(local_grads[2].astype(jnp.bfloat16), 'shard', scatter_di...  63 us
    reduce_scatter x1, waiting for transfers between devices, per_device(): lax.psum_scatter(local_grads[3].astype(jnp.bfloat16), 'shard', scatter_di...  62.9 us
    convert_element_type x2, other arithmetic, one_block(): grad_scores = (probs * (grad_probs - row_inner)).astype(jnp.bfloat16)  42.9 us
    unnamed x116, local copies, waits for them, and re-layouts  41.2 us
    dot_general x4, matrix products, block_scores(): jnp.einsum('qhd,khd->hqk', query_block, keys_seq, preferred_element_type=...  40.4 us
    dot_general x1, matrix products, per_device(): jnp.dot(normed_low, whole_up, preferred_element_type=jnp.float32)  38.1 us
  transfers between devices with their start and end apart: 11, of which 8 were waited for; matrix products, arithmetic and copies ran while one was open for 22% of the time, Pallas kernels for 0%

commit v1 on v0

v1 whole, which is shorter than its diff:
```python
import functools

import jax
import jax.numpy as jnp
from jax import lax
from jax.experimental import pallas as pl
from jax.experimental.pallas import tpu as pltpu
from jax.sharding import PartitionSpec as P

HEADS = 12
HEAD_DIM = 64
PAIR = 2 * HEAD_DIM

epsilon = 1e-12
masked_score = -1000000000.0
F32 = jnp.float32
BF16 = jnp.bfloat16


def dot_last(left, right):
    return lax.dot_general(left, right, (((1,), (1,)), ((), ())), preferred_element_type=F32)


def dot_plain(left, right):
    return lax.dot_general(left, right, (((1,), (0,)), ((), ())), preferred_element_type=F32)


def masked_keys(keys, length, head):
    lane = lax.broadcasted_iota(jnp.int32, keys.shape, 1)
    row = lax.broadcasted_iota(jnp.int32, keys.shape, 0)
    extra = jnp.where(row < length, 0.0, masked_score)
    return jnp.where(lane == (1 - head) * HEAD_DIM, extra, keys.astype(F32)).astype(BF16)


def head_lanes(block, head):
    lane = lax.broadcasted_iota(jnp.int32, block.shape, 1)
    inside = (lane >= head * HEAD_DIM) & (lane < (head + 1) * HEAD_DIM)
    return jnp.where(inside, block, 0.0)


def with_mask_lane(query, head):
    lane = lax.broadcasted_iota(jnp.int32, query.shape, 1)
    return jnp.where(lane == (1 - head) * HEAD_DIM, 1.0, query)


def forward_kernel(rows, length_ref, q_ref, k_ref, v_ref, out_ref, lse_ref, keys_aug, v_turned):
    seq = q_ref.shape[0]
    length = length_ref[pl.program_id(0)]
    for head in range(2):
        keys_aug[head] = masked_keys(k_ref[...], length, head)
    v_turned[...] = v_ref[...].T

    def block(index, _):
        span = pl.ds(pl.multiple_of(index * rows, rows), rows)
        scaled = q_ref[span, :].astype(F32) * HEAD_DIM ** (-0.5)
        parts = []
        for head in range(2):
            query = with_mask_lane(head_lanes(scaled, head), head).astype(BF16)
            scores = dot_last(keys_aug[head], query)
            top = jnp.max(scores, 0, keepdims=True)
            exponent = jnp.exp(scores - top)
            total = jnp.sum(exponent, 0, keepdims=True)
            mixed = dot_plain(
                v_turned[head * HEAD_DIM : (head + 1) * HEAD_DIM, :], exponent.astype(BF16)
            )
            parts.append(mixed / total)
            lse_ref[0, 0, pl.ds(head, 1), span] = top + jnp.log(total)
        out_ref[span, :] = jnp.concatenate(parts, 0).T.astype(BF16)
        return 0

    lax.fori_loop(0, seq // rows, block, 0)


def backward_kernel(
    rows,
    length_ref,
    q_ref,
    k_ref,
    v_ref,
    o_ref,
    do_ref,
    lse_ref,
    dq_ref,
    dk_ref,
    dv_ref,
    keys_aug,
    k_turned,
    dk_sum,
    dv_sum,
):
    seq = q_ref.shape[0]
    length = length_ref[pl.program_id(0)]
    for head in range(2):
        keys_aug[head] = masked_keys(k_ref[...], length, head)
    k_turned[...] = k_ref[...].T
    dk_sum[...] = jnp.zeros_like(dk_sum)
    dv_sum[...] = jnp.zeros_like(dv_sum)

    def block(index, _):
        span = pl.ds(pl.multiple_of(index * rows, rows), rows)
        scaled = q_ref[span, :].astype(F32) * HEAD_DIM ** (-0.5)
        grad = do_ref[span, :].astype(F32)
        product = (grad * o_ref[span, :].astype(F32)).T
        parts = []
        for head in range(2):
            lo, hi = head * HEAD_DIM, (head + 1) * HEAD_DIM
            alone = head_lanes(scaled, head)
            query = with_mask_lane(alone, head).astype(BF16)
            grad_low = head_lanes(grad, head).astype(BF16)
            inner = jnp.sum(product[lo:hi], 0, keepdims=True)
            lse = lse_ref[0, 0, pl.ds(head, 1), span]
            probs = jnp.exp(dot_last(keys_aug[head], query) - lse)
            dv_sum[...] += dot_plain(probs.astype(BF16), grad_low)
            grad_probs = dot_last(v_ref[...], grad_low)
            grad_scores = (probs * (grad_probs - inner)).astype(BF16)
            dk_sum[...] += dot_plain(grad_scores, alone.astype(BF16))
            parts.append(dot_plain(k_turned[lo:hi, :], grad_scores))
        dq_ref[span, :] = (jnp.concatenate(parts, 0).T * HEAD_DIM ** (-0.5)).astype(BF16)
        return 0

    lax.fori_loop(0, seq // rows, block, 0)
    dk_ref[...] = dk_sum[...].astype(BF16)
    dv_ref[...] = dv_sum[...].astype(BF16)


def column_spec(seq, offset):
    return pl.BlockSpec((seq, PAIR), lambda slot, pair: (slot, offset + pair))


def attention_forward(qkv_low, lengths, seq):
    tokens = qkv_low.shape[0]
    slots, pairs = tokens // seq, HEADS // 2
    return pl.pallas_call(
        functools.partial(forward_kernel, min(256, seq)),
        grid=(slots, pairs),
        in_specs=[
            pl.BlockSpec(memory_space=pltpu.SMEM),
            column_spec(seq, 0),
            column_spec(seq, pairs),
            column_spec(seq, 2 * pairs),
        ],
        out_specs=[
            column_spec(seq, 0),
            pl.BlockSpec((1, 1, 2, seq), lambda slot, pair: (slot, pair, 0, 0)),
        ],
        out_shape=[
            jax.ShapeDtypeStruct((tokens, HEADS * HEAD_DIM), BF16),
            jax.ShapeDtypeStruct((slots, pairs, 2, seq), F32),
        ],
        scratch_shapes=[pltpu.VMEM((2, seq, PAIR), BF16), pltpu.VMEM((PAIR, seq), BF16)],
        compiler_params=pltpu.CompilerParams(vmem_limit_bytes=48 * 2**20),
        cost_estimate=pl.CostEstimate(
            flops=16 * tokens * seq * HEADS * HEAD_DIM,
            bytes_accessed=8 * tokens * HEADS * HEAD_DIM,
            transcendentals=tokens * seq * HEADS,
        ),
        name="attention_forward",
    )(lengths, qkv_low, qkv_low, qkv_low)


def attention_backward(qkv_low, attended, d_attended, log_total, lengths, seq):
    tokens = qkv_low.shape[0]
    slots, pairs = tokens // seq, HEADS // 2
    grad_shape = jax.ShapeDtypeStruct((tokens, HEADS * HEAD_DIM), BF16)
    return pl.pallas_call(
        functools.partial(backward_kernel, min(256, seq)),
        grid=(slots, pairs),
        in_specs=[
            pl.BlockSpec(memory_space=pltpu.SMEM),
            column_spec(seq, 0),
            column_spec(seq, pairs),
            column_spec(seq, 2 * pairs),
            column_spec(seq, 0),
            column_spec(seq, 0),
            pl.BlockSpec((1, 1, 2, seq), lambda slot, pair: (slot, pair, 0, 0)),
        ],
        out_specs=[column_spec(seq, 0)] * 3,
        out_shape=[grad_shape] * 3,
        scratch_shapes=[
            pltpu.VMEM((2, seq, PAIR), BF16),
            pltpu.VMEM((PAIR, seq), BF16),
            pltpu.VMEM((seq, PAIR), F32),
            pltpu.VMEM((seq, PAIR), F32),
        ],
        compiler_params=pltpu.CompilerParams(vmem_limit_bytes=48 * 2**20),
        cost_estimate=pl.CostEstimate(
            flops=40 * tokens * seq * HEADS * HEAD_DIM,
            bytes_accessed=16 * tokens * HEADS * HEAD_DIM,
            transcendentals=tokens * seq * HEADS,
        ),
        name="attention_backward",
    )(lengths, qkv_low, qkv_low, qkv_low, attended, d_attended, log_total)


def swap(block, axis, count, bit):
    return lax.ppermute(block, axis, [(i, i ^ bit) for i in range(count)])


def bits_of(count):
    return [1 << i for i in range(count.bit_length() - 1)]


def join(mine, other, upper):
    return jnp.concatenate([jnp.where(upper, other, mine), jnp.where(upper, mine, other)], 0)


def after(value, earlier):
    return lax.optimization_barrier((value, earlier))[0]


def gather_shards(block, n_shard):
    me = lax.axis_index("shard")
    held = block[None]
    for bit in bits_of(n_shard):
        held = join(held, swap(held, "shard", n_shard, bit), (me & bit) != 0)
    return held


def gather_weight(piece, n_rep, n_shard, earlier):
    core = lax.axis_index("rep") & 1
    halves = piece.reshape(2, piece.shape[0] // 2, piece.shape[1])
    mine = lax.dynamic_index_in_dim(halves, core, 0, keepdims=False)
    if earlier is not None:
        mine = after(mine, earlier)
    held = gather_shards(mine, n_shard)
    other = swap(held, "rep", n_rep, 1)
    upper = core != 0
    whole = jnp.stack([jnp.where(upper, other, held), jnp.where(upper, held, other)], 1)
    return whole.reshape(n_shard * piece.shape[0], piece.shape[1]), held


def add_low(left, right):
    return (left.astype(F32) + right.astype(F32)).astype(BF16)


def halve(block, axis, count, bit, position):
    upper = (lax.axis_index(axis) & bit) != 0
    index = upper.astype(jnp.int32)
    keep = lax.dynamic_index_in_dim(block, index, position, keepdims=False)
    send = lax.dynamic_index_in_dim(block, 1 - index, position, keepdims=False)
    return add_low(keep, swap(send, axis, count, bit))


def reduce_gradient(grad, n_rep, n_shard):
    rows, cols = grad.shape
    rep = lax.axis_index("rep")
    part = rows // (2 * n_shard)
    held = halve(grad.reshape(n_shard, 2, part, cols), "rep", n_rep, 1, 1)
    for bit in reversed(bits_of(n_shard)):
        held = halve(
            held.reshape(2, held.shape[0] // 2, part, cols), "shard", n_shard, bit, 0
        )
    held = held[0]
    rest = bits_of(n_rep)[1:]
    for bit in rest:
        held = halve(held.reshape(2, held.shape[0] // 2, cols), "rep", n_rep, bit, 0)
    for bit in reversed(rest):
        held = join(held, swap(held, "rep", n_rep, bit), (rep & bit) != 0)
    return join(held, swap(held, "rep", n_rep, 1), (rep & 1) != 0).astype(F32)


def norm_forward(resid, gain_row, shift_row):
    center = resid - jnp.mean(resid, -1, keepdims=True)
    rstd_rows = lax.rsqrt(jnp.mean(center * center, -1, keepdims=True) + epsilon)
    normed = center * rstd_rows
    return (normed * gain_row + shift_row, normed, rstd_rows)


def norm_backward(grad_in, normed, rstd_rows, gain_row):
    scaled = grad_in * gain_row
    inner_term = (
        scaled
        - jnp.mean(scaled, -1, keepdims=True)
        - normed * jnp.mean(scaled * normed, -1, keepdims=True)
    )
    return (rstd_rows * inner_term, jnp.sum(grad_in * normed, 0), jnp.sum(grad_in, 0))


def gelu_pair(values):
    cdf = 0.5 + 0.5 * lax.erf(values * 0.7071067811865476)
    slope = cdf + values * (0.3989422804014327 * jnp.exp(-0.5 * values * values))
    return (values * cdf).astype(BF16), slope.astype(BF16)


def per_device(
    n_rep,
    n_shard,
    tokens,
    cotangent,
    lengths,
    w_qkv,
    w_out,
    w_up,
    w_down,
    norm_gains,
    biases,
    up_bias,
):
    width = tokens.shape[1]
    seq_len = tokens.shape[0] // lengths.shape[0]
    piece = width // n_shard
    gains, shifts = norm_gains.shape[0], biases.shape[0]
    small = jnp.concatenate([norm_gains.reshape(-1), biases.reshape(-1), up_bias])
    small_all = gather_shards(small[None], n_shard)[:, 0].astype(F32)
    cut = gains * piece
    end = cut + shifts * piece
    gain_f = jnp.swapaxes(small_all[:, :cut].reshape(n_shard, gains, piece), 0, 1)
    gain_f = gain_f.reshape(gains, width)
    bias_f = jnp.swapaxes(small_all[:, cut:end].reshape(n_shard, shifts, piece), 0, 1)
    bias_f = bias_f.reshape(shifts, width)
    upb_f = small_all[:, end:].reshape(-1)

    whole_qkv, mark = gather_weight(w_qkv, n_rep, n_shard, small_all)
    whole_out, mark = gather_weight(w_out, n_rep, n_shard, mark)
    whole_up, mark = gather_weight(w_up, n_rep, n_shard, mark)
    whole_down, mark = gather_weight(w_down, n_rep, n_shard, mark)

    qkv_bias = jnp.concatenate([bias_f[0], jnp.zeros_like(bias_f[0]), bias_f[1]])
    qkv_low = (jnp.dot(tokens, whole_qkv, preferred_element_type=F32) + qkv_bias).astype(BF16)
    attended_low, log_total = attention_forward(qkv_low, lengths, seq_len)
    branch = jnp.dot(attended_low, whole_out, preferred_element_type=F32) + bias_f[2]
    normed_first, unit_first, rstd_first = norm_forward(
        tokens.astype(F32) + branch, gain_f[0], bias_f[4]
    )
    normed_low = normed_first.astype(BF16)
    hidden_pre = jnp.dot(normed_low, whole_up, preferred_element_type=F32) + upb_f
    act_low, slope_low = gelu_pair(hidden_pre)
    mlp_out = jnp.dot(act_low, whole_down, preferred_element_type=F32) + bias_f[3]
    result, unit_second, rstd_second = norm_forward(normed_first + mlp_out, gain_f[1], bias_f[5])
    encoded = result.astype(BF16)

    d_second, d_gain_two, d_shift_two = norm_backward(
        cotangent.astype(F32), unit_second, rstd_second, gain_f[1]
    )
    d_mlp = d_second.astype(BF16)
    d_bias_down = jnp.sum(d_mlp.astype(F32), 0)
    grad_down = jnp.einsum("tf,td->fd", act_low, d_mlp, preferred_element_type=F32).astype(BF16)
    d_mlp = after(d_mlp, grad_down)
    d_act = jnp.einsum("td,fd->tf", d_mlp, whole_down, preferred_element_type=F32)
    d_pre = (d_act * slope_low.astype(F32)).astype(BF16)
    grad_up_bias = jnp.sum(d_pre.astype(F32), 0)
    grad_up = jnp.einsum("td,tf->df", normed_low, d_pre, preferred_element_type=F32).astype(BF16)
    d_pre = after(d_pre, grad_up)
    d_normed = d_second + jnp.einsum("tf,df->td", d_pre, whole_up, preferred_element_type=F32)
    d_first, d_gain_one, d_shift_one = norm_backward(d_normed, unit_first, rstd_first, gain_f[0])
    d_branch = d_first.astype(BF16)
    d_bias_out = jnp.sum(d_branch.astype(F32), 0)
    grad_out = jnp.einsum("ta,td->ad", attended_low, d_branch, preferred_element_type=F32)
    grad_out = grad_out.astype(BF16)
    d_branch = after(d_branch, grad_out)
    d_attended = jnp.einsum("td,ad->ta", d_branch, whole_out, preferred_element_type=F32)
    d_query, d_keys, d_values = attention_backward(
        qkv_low, attended_low, d_attended.astype(BF16), log_total, lengths, seq_len
    )
    d_qkv = jnp.concatenate([d_query, d_keys, d_values], axis=1)
    grad_qkv = jnp.einsum("td,te->de", tokens, d_qkv, preferred_element_type=F32).astype(BF16)
    d_qkv = after(d_qkv, grad_qkv)
    d_qkv_sums = jnp.sum(d_qkv.astype(F32), 0)
    grad_tokens = (
        d_first + jnp.einsum("te,de->td", d_qkv, whole_qkv, preferred_element_type=F32)
    ).astype(BF16)

    sum_down = reduce_gradient(grad_down, n_rep, n_shard)
    sum_up = reduce_gradient(grad_up, n_rep, n_shard)
    sum_out = reduce_gradient(grad_out, n_rep, n_shard)
    sum_qkv = reduce_gradient(grad_qkv, n_rep, n_shard)

    rows = [
        d_gain_one,
        d_gain_two,
        d_qkv_sums[:width],
        d_qkv_sums[2 * width :],
        d_bias_out,
        d_bias_down,
        d_shift_one,
        d_shift_two,
    ]
    small_sum = lax.psum(jnp.concatenate(rows + [grad_up_bias]), ("rep", "shard"))
    me = lax.axis_index("shard")
    table = small_sum[: len(rows) * width].reshape(len(rows), width)
    table = lax.dynamic_slice_in_dim(table, me * piece, piece, 1)
    up_piece = lax.dynamic_slice_in_dim(
        small_sum[len(rows) * width :], me * up_bias.shape[0], up_bias.shape[0], 0
    )
    return (
        encoded,
        grad_tokens,
        sum_qkv,
        sum_out,
        sum_up,
        sum_down,
        table[:gains],
        table[gains:],
        up_piece,
    )


def solution(mesh):
    both = P(("rep", "shard"), None)
    rows = P("shard", None)
    columns = P(None, "shard")
    in_specs = (both, both, P(("rep", "shard")), rows, rows, rows, rows, columns, columns, P("shard"))
    out_specs = (both, both, rows, rows, rows, rows, columns, columns, P("shard"))
    return jax.shard_map(
        functools.partial(per_device, mesh.shape["rep"], mesh.shape["shard"]),
        mesh=mesh,
        in_specs=in_specs,
        out_specs=out_specs,
        check_vma=False,
    )
```

time: 869 us -> 541 us (0.62)
  matrix products: 301 us -> 90.3 us
  waiting for transfers between devices: 303 us -> 176 us
  Pallas kernels: 0 us -> 91 us
  other arithmetic: 93.6 us -> 47.8 us
  blocking collectives: 83 us -> 44.9 us
  starting transfers between devices: 0.44 us -> 38.3 us
  local copies, waits for them, and re-layouts: 68.3 us -> 40.8 us
  between operations: 15.4 us -> 2.77 us
    dot_general x26 -> x12, matrix products: 301 us -> 90.3 us  [the longest x1 18.1 us: per_device(): jnp.einsum('td,tf->df', normed_low, d_pre, preferred_element_type=F32)]
    ppermute x0 -> x45, waiting for transfers between devices: none -> 176 us  [swap(): return lax.ppermute(block, axis, [(i, i ^ bit) for i in range(count)])]
    reduce_scatter x3 -> x0, waiting for transfers between devices: 147 us -> none  [the longest x1 63 us: per_device(): lax.psum_scatter(local_grads[2].astype(jnp.bfloat16), 'shard', scatter_di...]
    pallas_call x0 -> x2, Pallas kernels: none -> 91 us  [the longest x1 48.7 us: attention_backward(): pl.pallas_call(functools.partial(backward_kernel, min(256, seq)), grid=(s...]
    psum x1 -> x0, waiting for transfers between devices: 89.9 us -> none  [per_device(): lax.psum(owned[0].astype(jnp.bfloat16), 'rep').astype(jnp.float32)]
    all_gather x4 -> x0, waiting for transfers between devices: 45.3 us -> none  [the longest x1 32.4 us: per_device(): lax.all_gather(params_all[0], 'shard', axis=0, tiled=True)]
    ppermute x0 -> x45, starting transfers between devices: none -> 38.3 us  [swap(): return lax.ppermute(block, axis, [(i, i ^ bit) for i in range(count)])]
    convert_element_type x11 -> x25, other arithmetic: 52.9 us -> 17.7 us  [the longest x20 9.21 us: add_low(): return (left.astype(F32) + right.astype(F32)).astype(BF16)]
  transfers between devices with their start and end apart: 11 -> 45, of which waited for: 8 -> 25; matrix products, arithmetic and copies ran while one was open for 22% -> 16% of each run, Pallas kernels for 0% -> 8%
where the time goes in v1:
time: 541 us; the launch traced here: 532 us
  waiting for transfers between devices  176 us (33%)
  Pallas kernels  91 us (17%)
  matrix products  90.3 us (17%)
  other arithmetic  47.8 us (9%)
  blocking collectives  44.9 us (8%)
  local copies, waits for them, and re-layouts  40.8 us (8%)
  starting transfers between devices  38.3 us (7%)
    ppermute x45, waiting for transfers between devices, swap(): return lax.ppermute(block, axis, [(i, i ^ bit) for i in range(count)])  176 us
    pallas_call x1, Pallas kernels, attention_backward(): pl.pallas_call(functools.partial(backward_kernel, min(256, seq)), grid=(s...  48.7 us
    psum x1, blocking collectives, per_device(): lax.psum(jnp.concatenate(rows + [grad_up_bias]), ('rep', 'shard'))  44.9 us
    pallas_call x1, Pallas kernels, attention_forward(): pl.pallas_call(functools.partial(forward_kernel, min(256, seq)), grid=(sl...  42.2 us
    ppermute x45, starting transfers between devices, swap(): return lax.ppermute(block, axis, [(i, i ^ bit) for i in range(count)])  38.3 us
    unnamed x70, local copies, waits for them, and re-layouts  24.5 us
    dot_general x1, matrix products, per_device(): jnp.einsum('td,tf->df', normed_low, d_pre, preferred_element_type=F32)  18.1 us
    dot_general x1, matrix products, per_device(): jnp.einsum('td,fd->tf', d_mlp, whole_down, preferred_element_type=F32)  13.5 us
  transfers between devices with their start and end apart: 45, of which 25 were waited for; matrix products, arithmetic and copies ran while one was open for 16% of the time, Pallas kernels for 8%

profile of v1, /device:TPU:0, one launch (start us, length us, event | category | flops | bytes accessed | tf_op | source)
XLA Modules:
  0.0 532.3 jit_solution(10389018072813150903)
XLA Ops:
  10.9 18.7 %collective-permute-done.1 = bf16[1,192,2304]{2,1,0:T(8,128)(2,1)S(1)} collective-permute-done((bf16[1,192,2304]{2,1,0:T(8,128)(2,1)}, bf16[1,192,2304]{2,1,0:T(8,128)(2,1)S(1)}, u32[]{:S(2)}, u32[]{:S(2)}) %collective-permute-start.1) | collective-permute-done | bytes 884768 | tf_op jit(solution)/shard_map/ppermute | solution.py:196
  34.2 5.7 %collective-permute-done.3 = bf16[1,192,768]{2,1,0:T(8,128)(2,1)S(1)} collective-permute-done((bf16[1,192,768]{2,1,0:T(8,128)(2,1)S(1)}, bf16[1,192,768]{2,1,0:T(8,128)(2,1)S(1)}, u32[]{:S(2)}, u32[]{:S(2)}) %collective-permute-start.3) | collective-permute-done | bytes 294944 | tf_op jit(solution)/shard_map/ppermute | solution.py:196
  49.7 17.1 %collective-permute-done.5 = bf16[1,192,3072]{2,1,0:T(8,128)(2,1)} collective-permute-done((bf16[1,192,3072]{2,1,0:T(8,128)(2,1)}, bf16[1,192,3072]{2,1,0:T(8,128)(2,1)}, u32[]{:S(2)}, u32[]{:S(2)}) %collective-permute-start.5) | collective-permute-done | bytes 1179680 | tf_op jit(solution)/shard_map/ppermute | solution.py:196
  74.8 5.4 %fusion.5.q_ref.k_ref.v_ref = bf16[1024,2304]{1,0:T(8,128)(2,1)} fusion(bf16[1024,768]{1,0:T(8,128)(2,1)S(1)} %copy-done.11, bf16[768,2304]{1,0:T(8,128)(2,1)S(1)} %bitcast.203, f32[2304]{0:T(1024)S(1)} %pad_maximum_fusion.20), kind=kOutput, calls=%fused_computation.15 | convolution fusion | flops 3628597248 | bytes 9839616 | tf_op jit(solution)/shard_map/dot_general | solution.py:319
  80.2 42.2 %attention_forward.1 = (bf16[1024,768]{1,0:T(8,128)(2,1)S(1)}, f32[1,6,2,1024]{3,2,1,0:T(2,128)S(1)}) custom-call(s32[1]{0:T(128)S(6)} %copy.54.length_ref, bf16[1024,2304]{1,0:T(8,128)(2,1)} %fusion.5.q_ref.k_ref.v_ref, bf16[1024,2304]{1,0:T(8,128)(2,1)} %fusion.5.q_ref.k_ref.v_ref, bf16[1024,2304]{1,0:T(8,128)(2,1)} %fusion.5.q_ref.k_ref.v_ref), custom_call_target="tpu_custom_call" | custom-call | flops 12884901888 | bytes 6291456 | tf_op jit(solution)/shard_map/attention_forward/pallas_call | solution.py:133
  128.7 11.6 %multiply_convert_fusion.1 = (bf16[1024,3072]{1,0:T(8,128)(2,1)}, f32[1024,3072]{1,0:T(8,128)}) fusion(f32[3072]{0:T(1024)S(1)} %add.265, bf16[768,3072]{1,0:T(8,128)(2,1)S(1)} %bitcast.193, f32[1024,768]{0,1:T(8,128)S(1)} %get-tuple-element.125, f32[768]{0:T(1024)S(1)} %add.262, f32[768]{0:T(1024)S(1)} %mul.136, f32[1024]{0:T(1024)S(1)} %add_rsqrt_fusion.1, ...), kind=kOutput, calls=%fused_computation.8 | convolution fusion | flops 4854644736 | bytes 26765312 | tf_op jit(solution)/shard_map/dot_general | solution.py:326
  144.9 8.9 %fusion.39 = (f32[1024]{0:T(1024)S(1)}, f32[1024,768]{0,1:T(8,128)S(1)}) fusion(f32[768]{0:T(1024)S(1)} %add.269, bf16[1024,3072]{1,0:T(8,128)(2,1)} %get-tuple-element.126, bf16[3072,768]{1,0:T(8,128)(2,1)} %bitcast.195, f32[768]{0:T(1024)S(1)} %add.262, f32[768]{0:T(1024)S(1)} %mul.136, f32[1024]{0:T(1024)S(1)} %add_rsqrt_fusion.1, ...), kind=kOutput, calls=%fused_computation.216 | convolution fusion | flops 4837342208 | bytes 17323008 | tf_op jit(solution)/shard_map/dot_general | solution.py:328
  157.3 9.8 %convolution_convert_fusion.1 = bf16[3072,768]{1,0:T(8,128)(2,1)} fusion(bf16[1024,3072]{1,0:T(8,128)(2,1)} %get-tuple-element.126, bf16[1024,768]{0,1:T(8,128)(2,1)S(1)} %get-tuple-element.27), kind=kOutput, calls=%fused_computation.13 | convolution fusion | flops 4834197504 | bytes 12582912 | tf_op jit(solution)/shard_map/tf,td->fd/dot_general | solution.py:337
  167.2 13.5 %convert_reduce_fusion = (f32[3072]{0:T(1024)S(1)}, bf16[1024,3072]{1,0:T(8,128)(2,1)}) fusion(f32[1024,3072]{1,0:T(8,128)} %get-tuple-element.127, f32[3072]{0:T(1024)S(1)} %add.265, bf16[1024,768]{0,1:T(8,128)(2,1)S(1)} %get-tuple-element.27, bf16[3072,768]{1,0:T(8,128)(2,1)S(1)} %bitcast.198), kind=kOutput, calls=%fused_computation.6 | convolution fusion | flops 4879021056 | bytes 25190400 | tf_op jit(solution)/shard_map/td,fd->tf/dot_general | solution.py:339
  180.7 18.1 %convolution_convert_fusion = bf16[768,3072]{1,0:T(8,128)(2,1)} fusion(bf16[1024,3072]{1,0:T(8,128)(2,1)} %get-tuple-element.28, f32[1024,768]{0,1:T(8,128)S(1)} %get-tuple-element.125, f32[768]{0:T(1024)S(1)} %add.262, f32[768]{0:T(1024)S(1)} %mul.136, f32[1024]{0:T(1024)S(1)} %add_rsqrt_fusion.1, f32[1024]{0:T(1024)S(1)} %broadcast_multiply_fusion.5), kind=kOutput, calls=%fused_computation.12 | convolution fusion | flops 4838129664 | bytes 14170112 | tf_op jit(solution)/shard_map/td,tf->df/dot_general | solution.py:342
  198.9 6.4 %multiply_reduce_fusion = (f32[768]{0:T(1024)S(1)}, f32[1024]{0:T(1024)S(1)}, f32[1024]{0:T(1024)S(1)}, f32[768]{0:T(1024)S(1)}, f32[1024,768]{0,1:T(8,128)S(1)}) fusion(f32[1024,768]{0,1:T(8,128)S(1)} %get-tuple-element.125, f32[1024]{0:T(1024)S(1)} %add_rsqrt_fusion.1, f32[1024]{0:T(1024)S(1)} %broadcast_multiply_fusion.5, f32[768]{0:T(1024)S(1)} %mul.136, ...), kind=kOutput, calls=%fused_computation.37 | convolution fusion | flops 4845989888 | bytes 22065152 | tf_op jit(solution)/shard_map/tf,df->td/dot_general | solution.py:344
  212.0 48.7 %attention_backward.1 = (bf16[1024,768]{1,0:T(8,128)(2,1)S(1)}, bf16[1024,768]{1,0:T(8,128)(2,1)S(1)}, bf16[1024,768]{1,0:T(8,128)(2,1)S(1)}) custom-call(s32[1]{0:T(128)S(6)} %copy.54.length_ref, bf16[1024,2304]{1,0:T(8,128)(2,1)} %fusion.5.q_ref.k_ref.v_ref, bf16[1024,2304]{1,0:T(8,128)(2,1)} %fusion.5.q_ref.k_ref.v_ref, ...), custom_call_target="tpu_custom_call" | custom-call | flops 32212254720 | bytes 12582912 | tf_op jit(solution)/shard_map/attention_backward/pallas_call | solution.py:165
  271.3 5.3 add_convert_fusion.1
  321.4 44.9 %psum.7 = f32[9216]{0:T(1024)S(1)} all-reduce(f32[9216]{0:T(1024)} %constant_dynamic-update-slice_fusion.6), channel_id=1, replica_groups=mesh['rep'=16,'shard'=2] {'rep','shard'}, use_global_device_ids=true, to_apply=%region_16.17 | all-reduce | flops 9216 | bytes 73728 | tf_op jit(solution)/shard_map/psum | solution.py:378
  383.3 6.7 %collective-permute-done.11 = bf16[96,2304]{1,0:T(8,128)(2,1)S(1)} collective-permute-done((bf16[96,2304]{1,0:T(8,128)(2,1)S(1)}, bf16[96,2304]{1,0:T(8,128)(2,1)S(1)}, u32[]{:S(2)}, u32[]{:S(2)}) %collective-permute-start.11) | collective-permute-done | bytes 442400 | tf_op jit(solution)/shard_map/ppermute | solution.py:196
  404.9 6.1 %collective-permute-done.37 = bf16[1,768,768]{2,1,0:T(8,128)(2,1)S(1)} collective-permute-done((bf16[1,768,768]{2,1,0:T(8,128)(2,1)S(1)}, bf16[1,768,768]{2,1,0:T(8,128)(2,1)S(1)}, u32[]{:S(2)}, u32[]{:S(2)}) %collective-permute-start.37) | collective-permute-done | bytes 1179680 | tf_op jit(solution)/shard_map/ppermute | solution.py:196
  412.2 23.4 %collective-permute-done.28 = bf16[1,192,3072]{2,1,0:T(8,128)(2,1)S(1)} collective-permute-done((bf16[1,192,3072]{2,1,0:T(8,128)(2,1)S(1)}, bf16[1,192,3072]{2,1,0:T(8,128)(2,1)S(1)}, u32[]{:S(2)}, u32[]{:S(2)}) %collective-permute-start.28) | collective-permute-done | bytes 1179680 | tf_op jit(solution)/shard_map/ppermute | solution.py:196
  439.2 13.2 %collective-permute-done.29 = bf16[96,3072]{1,0:T(8,128)(2,1)S(1)} collective-permute-done((bf16[96,3072]{1,0:T(8,128)(2,1)S(1)}, bf16[96,3072]{1,0:T(8,128)(2,1)S(1)}, u32[]{:S(2)}, u32[]{:S(2)}) %collective-permute-start.29) | collective-permute-done | bytes 589856 | tf_op jit(solution)/shard_map/ppermute | solution.py:196
  453.2 7.0 %collective-permute-done.16 = bf16[96,2304]{1,0:T(8,128)(2,1)S(1)} collective-permute-done((bf16[96,2304]{1,0:T(8,128)(2,1)S(1)}, bf16[96,2304]{1,0:T(8,128)(2,1)S(1)}, u32[]{:S(2)}, u32[]{:S(2)}) %collective-permute-start.16) | collective-permute-done | bytes 442400 | tf_op jit(solution)/shard_map/ppermute | solution.py:196
  463.7 8.4 %collective-permute-done.40 = bf16[96,768]{1,0:T(8,128)(2,1)S(1)} collective-permute-done((bf16[96,768]{1,0:T(8,128)(2,1)S(1)}, bf16[96,768]{1,0:T(8,128)(2,1)S(1)}, u32[]{:S(2)}, u32[]{:S(2)}) %collective-permute-start.40) | collective-permute-done | bytes 147488 | tf_op jit(solution)/shard_map/ppermute | solution.py:196
  472.2 9.4 %collective-permute-done.31 = bf16[24,3072]{1,0:T(8,128)(2,1)S(1)} collective-permute-done((bf16[24,3072]{1,0:T(8,128)(2,1)S(1)}, bf16[24,3072]{1,0:T(8,128)(2,1)S(1)}, u32[]{:S(2)}, u32[]{:S(2)}) %collective-permute-start.31) | collective-permute-done | bytes 147488 | tf_op jit(solution)/shard_map/ppermute | solution.py:196
  488.5 6.2 %collective-permute-done.42 = bf16[192,768]{1,0:T(8,128)(2,1)S(1)} collective-permute-done((bf16[192,768]{1,0:T(8,128)(2,1)S(1)}, bf16[192,768]{1,0:T(8,128)(2,1)S(1)}, u32[]{:S(2)}, u32[]{:S(2)}) %collective-permute-start.42) | collective-permute-done | bytes 294944 | tf_op jit(solution)/shard_map/ppermute | solution.py:196
  502.3 8.8 %collective-permute-done.43 = bf16[384,768]{1,0:T(8,128)(2,1)S(1)} collective-permute-done((bf16[384,768]{1,0:T(8,128)(2,1)S(1)}, bf16[384,768]{1,0:T(8,128)(2,1)S(1)}, u32[]{:S(2)}, u32[]{:S(2)}) %collective-permute-start.43) | collective-permute-done | bytes 589856 | tf_op jit(solution)/shard_map/ppermute | solution.py:196
  511.5 11.2 %collective-permute-done.34 = bf16[96,3072]{1,0:T(8,128)(2,1)S(1)} collective-permute-done((bf16[96,3072]{1,0:T(8,128)(2,1)S(1)}, bf16[96,3072]{1,0:T(8,128)(2,1)S(1)}, u32[]{:S(2)}, u32[]{:S(2)}) %collective-permute-start.34) | collective-permute-done | bytes 589856 | tf_op jit(solution)/shard_map/ppermute | solution.py:196
  (293 shorter events, 172.6 us)
Async XLA Ops:
  8.2 21.4 %collective-permute-start.1 = (bf16[1,192,2304]{2,1,0:T(8,128)(2,1)}, bf16[1,192,2304]{2,1,0:T(8,128)(2,1)S(1)}, u32[]{:S(2)}, u32[]{:S(2)}) collective-permute-start(bf16[1,192,2304]{2,1,0:T(8,128)(2,1)} %bitcast.3), channel_id=1, source_target_pairs={{0,1},{1,0},{2,3},{3,2},{4,5},{5,4},{6,7},{7,6},{8,9},{9,8},{10,11... | collective-permute-start | bytes 2654216 | tf_op jit(solution)/shard_map/ppermute | solution.py:196
  40.9 25.9 %collective-permute-start.5 = (bf16[1,192,3072]{2,1,0:T(8,128)(2,1)}, bf16[1,192,3072]{2,1,0:T(8,128)(2,1)}, u32[]{:S(2)}, u32[]{:S(2)}) collective-permute-start(bf16[1,192,3072]{2,1,0:T(8,128)(2,1)} %bitcast.21), channel_id=1, source_target_pairs={{0,1},{1,0},{2,3},{3,2},{4,5},{5,4},{6,7},{7,6},{8,9},{9,8},{10,11... | collective-permute-start | bytes 3538952 | tf_op jit(solution)/shard_map/ppermute | solution.py:196
  47.7 22.8 %collective-permute-start.2 = (bf16[2,192,2304]{2,1,0:T(8,128)(2,1)}, bf16[2,192,2304]{2,1,0:T(8,128)(2,1)}, u32[]{:S(2)}, u32[]{:S(2)}) collective-permute-start(bf16[2,192,2304]{2,1,0:T(8,128)(2,1)} %pad_maximum_fusion.5), channel_id=1, source_target_pairs={{0,2},{2,0},{4,6},{6,4},{8,10},{10,8},{12,14},{14,12},{16,18},{18,... | collective-permute-start | bytes 5308424 | tf_op jit(solution)/shard_map/ppermute | solution.py:196
  70.2 56.0 %collective-permute-start.6 = (bf16[2,192,3072]{2,1,0:T(8,128)(2,1)}, bf16[2,192,3072]{2,1,0:T(8,128)(2,1)}, u32[]{:S(2)}, u32[]{:S(2)}) collective-permute-start(bf16[2,192,3072]{2,1,0:T(8,128)(2,1)} %pad_maximum_fusion.3), channel_id=1, source_target_pairs={{0,2},{2,0},{4,6},{6,4},{8,10},{10,8},{12,14},{14,12},{16,18},{18,... | collective-permute-start | bytes 7077896 | tf_op jit(solution)/shard_map/ppermute | solution.py:196
  70.2 54.3 %collective-permute-start.7 = (bf16[1,768,768]{2,1,0:T(8,128)(2,1)S(1)}, bf16[1,768,768]{2,1,0:T(8,128)(2,1)}, u32[]{:S(2)}, u32[]{:S(2)}) collective-permute-start(bf16[1,768,768]{2,1,0:T(8,128)(2,1)S(1)} %bitcast.182), channel_id=1, source_target_pairs={{0,1},{1,0},{2,3},{3,2},{4,5},{5,4},{6,7},{7,6},{8,9},{9,8},{10,11... | collective-permute-start | bytes 3538952 | tf_op jit(solution)/shard_map/ppermute | solution.py:196
  126.1 14.1 %collective-permute-start.8 = (bf16[2,768,768]{2,1,0:T(8,128)(2,1)S(1)}, bf16[2,768,768]{2,1,0:T(8,128)(2,1)}, u32[]{:S(2)}, u32[]{:S(2)}) collective-permute-start(bf16[2,768,768]{2,1,0:T(8,128)(2,1)S(1)} %pad_maximum_fusion.4), channel_id=1, source_target_pairs={{0,2},{2,0},{4,6},{6,4},{8,10},{10,8},{12,14},{14,12},{16,18},{18,... | collective-permute-start | bytes 7077896 | tf_op jit(solution)/shard_map/ppermute | solution.py:196
  268.5 110.6 %collective-permute-start.36 = (bf16[2,768,768]{2,1,0:T(8,128)(2,1)}, bf16[2,768,768]{2,1,0:T(8,128)(2,1)}, u32[]{:S(2)}, u32[]{:S(2)}) collective-permute-start(bf16[2,768,768]{2,1,0:T(8,128)(2,1)} %dynamic-slice_bitcast_fusion), channel_id=1, source_target_pairs={{0,2},{2,0},{4,6},{6,4},{8,10},{10,8},{12,14},{14,12},{16,18},{18,... | collective-permute-start | bytes 7077896 | tf_op jit(solution)/shard_map/ppermute | solution.py:196
  269.3 45.2 %collective-permute-start.9 = (bf16[2,192,2304]{2,1,0:T(8,128)(2,1)S(1)}, bf16[2,192,2304]{2,1,0:T(8,128)(2,1)S(1)}, u32[]{:S(2)}, u32[]{:S(2)}) collective-permute-start(bf16[2,192,2304]{2,1,0:T(8,128)(2,1)S(1)} %dynamic-slice_bitcast_fusion.2), channel_id=1, source_target_pairs={{0,2},{2,0},{4,6},{6,4},{8,10},{10,8},{12,14},{14,12},{16,18},{18,... | collective-permute-start | bytes 5308424 | tf_op jit(solution)/shard_map/ppermute | solution.py:196
  315.9 59.4 %collective-permute-start.10 = (bf16[1,192,2304]{2,1,0:T(8,128)(2,1)}, bf16[1,192,2304]{2,1,0:T(8,128)(2,1)}, u32[]{:S(2)}, u32[]{:S(2)}) collective-permute-start(bf16[1,192,2304]{2,1,0:T(8,128)(2,1)} %constant_dynamic-slice_fusion.4), channel_id=1, source_target_pairs={{0,1},{1,0},{2,3},{3,2},{4,5},{5,4},{6,7},{7,6},{8,9},{9,8},{10,11... | collective-permute-start | bytes 2654216 | tf_op jit(solution)/shard_map/ppermute | solution.py:196
  319.5 53.6 %collective-permute-start.26 = (bf16[192,768]{1,0:T(8,128)(2,1)}, bf16[192,768]{1,0:T(8,128)(2,1)}, u32[]{:S(2)}, u32[]{:S(2)}) collective-permute-start(bf16[192,768]{1,0:T(8,128)(2,1)} %pad_maximum_fusion.14), channel_id=1, source_target_pairs={{0,2},{2,0},{4,6},{6,4},{8,10},{10,8},{12,14},{14,12},{16,18},{18,... | collective-permute-start | bytes 884744 | tf_op jit(solution)/shard_map/ppermute | solution.py:196
  367.0 23.7 %collective-permute-start.27 = (bf16[2,192,3072]{2,1,0:T(8,128)(2,1)}, bf16[2,192,3072]{2,1,0:T(8,128)(2,1)}, u32[]{:S(2)}, u32[]{:S(2)}) collective-permute-start(bf16[2,192,3072]{2,1,0:T(8,128)(2,1)} %dynamic-slice_bitcast_fusion.1), channel_id=1, source_target_pairs={{0,2},{2,0},{4,6},{6,4},{8,10},{10,8},{12,14},{14,12},{16,18},{18,... | collective-permute-start | bytes 7077896 | tf_op jit(solution)/shard_map/ppermute | solution.py:196
  376.9 13.1 %collective-permute-start.11 = (bf16[96,2304]{1,0:T(8,128)(2,1)S(1)}, bf16[96,2304]{1,0:T(8,128)(2,1)S(1)}, u32[]{:S(2)}, u32[]{:S(2)}) collective-permute-start(bf16[96,2304]{1,0:T(8,128)(2,1)S(1)} %dynamic-slice_bitcast_fusion.9), channel_id=1, source_target_pairs={{0,4},{2,6},{4,0},{6,2},{8,12},{10,14},{12,8},{14,10},{16,20},{18,... | collective-permute-start | bytes 1327112 | tf_op jit(solution)/shard_map/ppermute | solution.py:196
  382.1 28.9 %collective-permute-start.37 = (bf16[1,768,768]{2,1,0:T(8,128)(2,1)S(1)}, bf16[1,768,768]{2,1,0:T(8,128)(2,1)S(1)}, u32[]{:S(2)}, u32[]{:S(2)}) collective-permute-start(bf16[1,768,768]{2,1,0:T(8,128)(2,1)S(1)} %constant_dynamic-slice_fusion.1), channel_id=1, source_target_pairs={{0,1},{1,0},{2,3},{3,2},{4,5},{5,4},{6,7},{7,6},{8,9},{9,8},{10,11... | collective-permute-start | bytes 3538952 | tf_op jit(solution)/shard_map/ppermute | solution.py:196
  398.3 37.3 %collective-permute-start.28 = (bf16[1,192,3072]{2,1,0:T(8,128)(2,1)S(1)}, bf16[1,192,3072]{2,1,0:T(8,128)(2,1)S(1)}, u32[]{:S(2)}, u32[]{:S(2)}) collective-permute-start(bf16[1,192,3072]{2,1,0:T(8,128)(2,1)S(1)} %constant_dynamic-slice_fusion.2), channel_id=1, source_target_pairs={{0,1},{1,0},{2,3},{3,2},{4,5},{5,4},{6,7},{7,6},{8,9},{9,8},{10,11... | collective-permute-start | bytes 3538952 | tf_op jit(solution)/shard_map/ppermute | solution.py:196
  411.4 27.0 %collective-permute-start.38 = (bf16[384,768]{1,0:T(8,128)(2,1)S(1)}, bf16[384,768]{1,0:T(8,128)(2,1)S(1)}, u32[]{:S(2)}, u32[]{:S(2)}) collective-permute-start(bf16[384,768]{1,0:T(8,128)(2,1)S(1)} %dynamic-slice_bitcast_fusion.6), channel_id=1, source_target_pairs={{0,4},{2,6},{4,0},{6,2},{8,12},{10,14},{12,8},{14,10},{16,20},{18,... | collective-permute-start | bytes 1769480 | tf_op jit(solution)/shard_map/ppermute | solution.py:196
  411.5 24.9 %collective-permute-start.15 = (bf16[48,2304]{1,0:T(8,128)(2,1)S(1)}, bf16[48,2304]{1,0:T(8,128)(2,1)S(1)}, u32[]{:S(2)}, u32[]{:S(2)}) collective-permute-start(bf16[48,2304]{1,0:T(8,128)(2,1)S(1)} %pad_maximum_fusion.17), channel_id=1, source_target_pairs={{0,8},{2,10},{4,12},{6,14},{8,0},{10,2},{12,4},{14,6},{16,24},{18,... | collective-permute-start | bytes 663560 | tf_op jit(solution)/shard_map/ppermute | solution.py:196
  436.0 16.3 %collective-permute-start.29 = (bf16[96,3072]{1,0:T(8,128)(2,1)S(1)}, bf16[96,3072]{1,0:T(8,128)(2,1)S(1)}, u32[]{:S(2)}, u32[]{:S(2)}) collective-permute-start(bf16[96,3072]{1,0:T(8,128)(2,1)S(1)} %dynamic-slice_bitcast_fusion.7), channel_id=1, source_target_pairs={{0,4},{2,6},{4,0},{6,2},{8,12},{10,14},{12,8},{14,10},{16,20},{18,... | collective-permute-start | bytes 1769480 | tf_op jit(solution)/shard_map/ppermute | solution.py:196
  436.6 23.6 %collective-permute-start.16 = (bf16[96,2304]{1,0:T(8,128)(2,1)S(1)}, bf16[96,2304]{1,0:T(8,128)(2,1)S(1)}, u32[]{:S(2)}, u32[]{:S(2)}) collective-permute-start(bf16[96,2304]{1,0:T(8,128)(2,1)S(1)} %pad_maximum_fusion.13), channel_id=1, source_target_pairs={{0,4},{2,6},{4,0},{6,2},{8,12},{10,14},{12,8},{14,10},{16,20},{18,... | collective-permute-start | bytes 1327112 | tf_op jit(solution)/shard_map/ppermute | solution.py:196
  438.5 21.8 %collective-permute-start.39 = (bf16[192,768]{1,0:T(8,128)(2,1)S(1)}, bf16[192,768]{1,0:T(8,128)(2,1)S(1)}, u32[]{:S(2)}, u32[]{:S(2)}) collective-permute-start(bf16[192,768]{1,0:T(8,128)(2,1)S(1)} %dynamic-slice_bitcast_fusion.10), channel_id=1, source_target_pairs={{0,8},{2,10},{4,12},{6,14},{8,0},{10,2},{12,4},{14,6},{16,24},{18,... | collective-permute-start | bytes 884744 | tf_op jit(solution)/shard_map/ppermute | solution.py:196
  461.3 20.3 %collective-permute-start.31 = (bf16[24,3072]{1,0:T(8,128)(2,1)S(1)}, bf16[24,3072]{1,0:T(8,128)(2,1)S(1)}, u32[]{:S(2)}, u32[]{:S(2)}) collective-permute-start(bf16[24,3072]{1,0:T(8,128)(2,1)S(1)} %dynamic-slice_bitcast_fusion.15), channel_id=1, source_target_pairs={{0,16},{2,18},{4,20},{6,22},{8,24},{10,26},{12,28},{14,30},{16,0},... | collective-permute-start | bytes 442376 | tf_op jit(solution)/shard_map/ppermute | solution.py:196
  494.8 16.3 %collective-permute-start.43 = (bf16[384,768]{1,0:T(8,128)(2,1)S(1)}, bf16[384,768]{1,0:T(8,128)(2,1)S(1)}, u32[]{:S(2)}, u32[]{:S(2)}) collective-permute-start(bf16[384,768]{1,0:T(8,128)(2,1)S(1)} %pad_maximum_fusion.12), channel_id=1, source_target_pairs={{0,4},{2,6},{4,0},{6,2},{8,12},{10,14},{12,8},{14,10},{16,20},{18,... | collective-permute-start | bytes 1769480 | tf_op jit(solution)/shard_map/ppermute | solution.py:196
  501.1 21.6 %collective-permute-start.34 = (bf16[96,3072]{1,0:T(8,128)(2,1)S(1)}, bf16[96,3072]{1,0:T(8,128)(2,1)S(1)}, u32[]{:S(2)}, u32[]{:S(2)}) collective-permute-start(bf16[96,3072]{1,0:T(8,128)(2,1)S(1)} %pad_maximum_fusion.11), channel_id=1, source_target_pairs={{0,4},{2,6},{4,0},{6,2},{8,12},{10,14},{12,8},{14,10},{16,20},{18,... | collective-permute-start | bytes 1769480 | tf_op jit(solution)/shard_map/ppermute | solution.py:196
  502.2 20.9 %collective-permute-start.17 = (bf16[192,2304]{1,0:T(8,128)(2,1)S(1)}, bf16[192,2304]{1,0:T(8,128)(2,1)S(1)}, u32[]{:S(2)}, u32[]{:S(2)}) collective-permute-start(bf16[192,2304]{1,0:T(8,128)(2,1)S(1)} %pad_maximum_fusion.9), channel_id=1, source_target_pairs={{0,2},{2,0},{4,6},{6,4},{8,10},{10,8},{12,14},{14,12},{16,18},{18,... | collective-permute-start | bytes 2654216 | tf_op jit(solution)/shard_map/ppermute | solution.py:196
  511.4 14.1 %collective-permute-start.44 = (bf16[768,768]{1,0:T(8,128)(2,1)S(1)}, bf16[768,768]{1,0:T(8,128)(2,1)S(1)}, u32[]{:S(2)}, u32[]{:S(2)}) collective-permute-start(bf16[768,768]{1,0:T(8,128)(2,1)S(1)} %pad_maximum_fusion.8), channel_id=1, source_target_pairs={{0,2},{2,0},{4,6},{6,4},{8,10},{10,8},{12,14},{14,12},{16,18},{18,... | collective-permute-start | bytes 3538952 | tf_op jit(solution)/shard_map/ppermute | solution.py:196
  (49 other events, 541.4 us)
